TPU v7x, 32 devices: a whole 2x2x4 slice. The times are simulated.
32 devices in a mesh: gx: 8 (over y, x, core), gy: 4 (over z).
Axes of the slice: x: 2, y: 2, z: 4, core: 2. Of those that a mesh axis runs over, the one named last changes fastest.
Arguments:
- coefficients: float32 [8, 4, 256, 1024], P('gx', 'gy'), may hold values from -6 to 6
- transfer_blocks: float32 [4, 8, 4, 256, 512], P(None, 'gx', 'gy'), may hold values from -0.25 to 0.25
Outputs:
- result_blocks: float32 [8, 4, 256, 1024], P('gx', 'gy')
All inputs are finite; a program needn't handle non-finite values.
Results may differ from a plain program's by a relative error of at most 0.0001.
Values sent between devices are 32-bit elements; how exact they have to be, the bound alone decides.
A program may use at most 64 MiB of HBM per device.

v0:
```python
import jax
import jax.numpy as jnp
from jax import lax
from jax.sharding import PartitionSpec as P


def partner_2(block, axis, bit):
    count = lax.axis_size(axis)
    route = []
    for low in range(count):
        high = low | 1 << bit
        if high != low and high < count:
            route += [(low, high), (high, low)]
    return lax.ppermute(block, axis, route)


def matmul(left, right):
    return jnp.dot(left, right, preferred_element_type=jnp.float32, precision=lax.Precision.HIGHEST)


def swap_high_half(state, bit_number):
    return partner_2(state, "gx", bit_number)


def swap_low_half(state, bit_number):
    return partner_2(state, "gy", bit_number)


def one_level(state, block, swapper, bit_number, upper_bit):
    partner = swapper(state, bit_number)
    lower_block = jnp.where(upper_bit == 0, state, partner)
    upper_block = jnp.where(upper_bit == 0, partner, state)
    stacked = jnp.concatenate([lower_block, upper_block], axis=0)
    return matmul(block, stacked)


def on_device(coefficients, transfer_blocks):
    state = coefficients[0, 0]
    blocks = transfer_blocks[:, 0, 0]
    high_top = lax.axis_size("gx").bit_length() - 2
    low_top = lax.axis_size("gy").bit_length() - 2
    high_index = lax.axis_index("gx")
    low_index = lax.axis_index("gy")
    plan = [("high", high_top), ("low", low_top), ("high", high_top - 1), ("low", low_top - 1)]
    width = state.shape[1] // 2
    groups = [state[:, :width], state[:, width:]]
    for level_number in range(4):
        which, bit_number = plan[level_number]
        if which == "high":
            upper_bit = jnp.bitwise_and(jnp.right_shift(high_index, bit_number), 1)
            swapper = swap_high_half
        else:
            upper_bit = jnp.bitwise_and(jnp.right_shift(low_index, bit_number), 1)
            swapper = swap_low_half
        groups = [
            one_level(group, blocks[level_number], swapper, bit_number, upper_bit)
            for group in groups
        ]
    state = jnp.concatenate(groups, axis=1)
    return state[None, None]


def solution(mesh):
    in_specs = (P("gx", "gy", None, None), P(None, "gx", "gy", None, None))
    out_specs = P("gx", "gy", None, None)
    return jax.shard_map(
        on_device, mesh=mesh, in_specs=in_specs, out_specs=out_specs, check_vma=False
    )
```

profile of v0, /device:TPU:0, one launch (start us, length us, event | category | flops | bytes accessed | tf_op | source)
XLA Modules:
  0.0 102.7 jit_solution(15428816685295590347)
XLA Ops:
  0.0 0.0 copy-start
  0.0 2.0 %slice.32 = f32[256,512]{1,0:T(8,128)} slice(f32[256,1024]{1,0:T(8,128)} %bitcast.39), slice={[0:256], [0:512]} | slice | bytes 1048576 | tf_op jit(solution)/shard_map/slice | solution.py:46
  2.0 3.0 %collective-permute-start = (f32[256,512]{1,0:T(8,128)}, f32[256,512]{1,0:T(8,128)}, u32[]{:S(2)}, u32[]{:S(2)}) collective-permute-start(f32[256,512]{1,0:T(8,128)} %slice.32), channel_id=1, source_target_pairs={{0,16},{16,0},{4,20},{20,4},{8,24},{24,8},{12,28},{28,12},{1,17},{... | collective-permute-start | bytes 1572872 | tf_op jit(solution)/shard_map/ppermute | solution.py:14
  5.0 0.0 copy-start.1
  5.0 12.2 %collective-permute-done = f32[256,512]{1,0:T(8,128)} collective-permute-done((f32[256,512]{1,0:T(8,128)}, f32[256,512]{1,0:T(8,128)}, u32[]{:S(2)}, u32[]{:S(2)}) %collective-permute-start) | collective-permute-done | bytes 524320 | tf_op jit(solution)/shard_map/ppermute | solution.py:14
  17.2 2.6 %broadcast_select_fusion.3 = (f32[256,512]{1,0:T(8,128)}, f32[256,512]{1,0:T(8,128)}, f32[256,512]{1,0:T(8,128)}) fusion(f32[256,512]{1,0:T(8,128)} %collective-permute-done, pred[]{:T(512)S(6)} %eq.11, f32[256,1024]{1,0:T(8,128)} %bitcast.40), kind=kLoop, calls=%fused_computation.52 | loop fusion | flops 262144 | bytes 3145729 | tf_op jit(solution)/shard_map/jit(_where)/select_n | solution.py:31
  19.8 1.7 %collective-permute-start.4 = (f32[256,512]{1,0:T(8,128)}, f32[256,512]{1,0:T(8,128)}, u32[]{:S(2)}, u32[]{:S(2)}) collective-permute-start(f32[256,512]{1,0:T(8,128)} %get-tuple-element.15), channel_id=1, source_target_pairs={{0,16},{16,0},{4,20},{20,4},{8,24},{24,8},{12,28},{28,12},{1,17},{... | collective-permute-start | bytes 1572872 | tf_op jit(solution)/shard_map/ppermute | solution.py:14
  21.6 0.0 copy-done
  21.6 2.3 %convolution_bitcast_fusion.7 = f32[256,512]{1,0:T(8,128)S(1)} fusion(f32[256,512]{1,0:T(8,128)} %get-tuple-element.6, f32[256,512]{1,0:T(8,128)} %get-tuple-element.5, f32[4,1,1,256,512]{4,3,2,1,0:T(8,128)S(1)} %copy-done), kind=kOutput, calls=%fused_computation.7 | convolution fusion | flops 805568512 | bytes 2097152 | tf_op jit(solution)/shard_map/dot_general | solution.py:18
  23.9 2.7 %collective-permute-start.1 = (f32[256,512]{1,0:T(8,128)S(1)}, f32[256,512]{1,0:T(8,128)S(1)}, u32[]{:S(2)}, u32[]{:S(2)}) collective-permute-start(f32[256,512]{1,0:T(8,128)S(1)} %convolution_bitcast_fusion.7), channel_id=1, source_target_pairs={{0,2},{2,0},{1,3},{3,1},{4,6},{6,4},{5,7},{7,5},{8,10},{10,8},{9,1... | collective-permute-start | bytes 1572872 | tf_op jit(solution)/shard_map/ppermute | solution.py:14
  26.5 6.7 %collective-permute-done.4 = f32[256,512]{1,0:T(8,128)} collective-permute-done((f32[256,512]{1,0:T(8,128)}, f32[256,512]{1,0:T(8,128)}, u32[]{:S(2)}, u32[]{:S(2)}) %collective-permute-start.4) | collective-permute-done | bytes 524320 | tf_op jit(solution)/shard_map/ppermute | solution.py:14
  33.3 0.0 copy-done.1
  33.3 1.2 %broadcast_select_fusion.1 = (f32[256,512]{1,0:T(8,128)S(1)}, f32[256,512]{1,0:T(8,128)S(1)}) fusion(f32[256,512]{1,0:T(8,128)} %collective-permute-done.4, pred[]{:T(512)S(6)} %eq.11, f32[256,1024]{1,0:T(8,128)S(1)} %bitcast.41), kind=kLoop, calls=%fused_computation.50 | loop fusion | flops 262144 | bytes 2097153 | tf_op jit(solution)/shard_map/jit(_where)/select_n | solution.py:31
  34.4 1.1 %convolution_bitcast_fusion.3 = f32[256,512]{1,0:T(8,128)S(1)} fusion(f32[256,512]{1,0:T(8,128)S(1)} %get-tuple-element.8, f32[256,512]{1,0:T(8,128)S(1)} %get-tuple-element.7, f32[4,1,1,256,512]{4,3,2,1,0:T(8,128)S(1)} %copy-done), kind=kOutput, calls=%fused_computation.3 | convolution fusion | flops 805568512 | bytes 2097152 | tf_op jit(solution)/shard_map/dot_general | solution.py:18
  35.5 2.6 %collective-permute-start.5 = (f32[256,512]{1,0:T(8,128)S(1)}, f32[256,512]{1,0:T(8,128)S(1)}, u32[]{:S(2)}, u32[]{:S(2)}) collective-permute-start(f32[256,512]{1,0:T(8,128)S(1)} %convolution_bitcast_fusion.3), channel_id=1, source_target_pairs={{0,2},{2,0},{1,3},{3,1},{4,6},{6,4},{5,7},{7,5},{8,10},{10,8},{9,1... | collective-permute-start | bytes 1572872 | tf_op jit(solution)/shard_map/ppermute | solution.py:14
  38.1 22.9 %collective-permute-done.1 = f32[256,512]{1,0:T(8,128)S(1)} collective-permute-done((f32[256,512]{1,0:T(8,128)S(1)}, f32[256,512]{1,0:T(8,128)S(1)}, u32[]{:S(2)}, u32[]{:S(2)}) %collective-permute-start.1) | collective-permute-done | bytes 524320 | tf_op jit(solution)/shard_map/ppermute | solution.py:14
  61.0 0.1 broadcast_select_fusion.7
  61.1 1.1 %convolution_bitcast_fusion.6 = f32[256,512]{1,0:T(8,128)S(1)} fusion(f32[256,512]{1,0:T(8,128)S(1)} %get-tuple-element.14, f32[256,512]{1,0:T(8,128)S(1)} %get-tuple-element.13, f32[4,1,1,256,512]{4,3,2,1,0:T(8,128)S(1)} %copy-done), kind=kOutput, calls=%fused_computation.6 | convolution fusion | flops 805568512 | bytes 2097152 | tf_op jit(solution)/shard_map/dot_general | solution.py:18
  62.2 1.6 %collective-permute-start.2 = (f32[256,512]{1,0:T(8,128)S(1)}, f32[256,512]{1,0:T(8,128)S(1)}, u32[]{:S(2)}, u32[]{:S(2)}) collective-permute-start(f32[256,512]{1,0:T(8,128)S(1)} %convolution_bitcast_fusion.6), channel_id=1, source_target_pairs={{0,8},{8,0},{4,12},{12,4},{16,24},{24,16},{20,28},{28,20},{1,9},{9... | collective-permute-start | bytes 1572872 | tf_op jit(solution)/shard_map/ppermute | solution.py:14
  63.8 7.3 %collective-permute-done.5 = f32[256,512]{1,0:T(8,128)S(1)} collective-permute-done((f32[256,512]{1,0:T(8,128)S(1)}, f32[256,512]{1,0:T(8,128)S(1)}, u32[]{:S(2)}, u32[]{:S(2)}) %collective-permute-start.5) | collective-permute-done | bytes 524320 | tf_op jit(solution)/shard_map/ppermute | solution.py:14
  71.1 0.1 broadcast_select_fusion.5
  71.2 1.1 %convolution_bitcast_fusion.2 = f32[256,512]{1,0:T(8,128)S(1)} fusion(f32[256,512]{1,0:T(8,128)S(1)} %get-tuple-element.21, f32[256,512]{1,0:T(8,128)S(1)} %get-tuple-element.20, f32[4,1,1,256,512]{4,3,2,1,0:T(8,128)S(1)} %copy-done), kind=kOutput, calls=%fused_computation.2 | convolution fusion | flops 805568512 | bytes 2097152 | tf_op jit(solution)/shard_map/dot_general | solution.py:18
  72.3 1.6 %collective-permute-start.6 = (f32[256,512]{1,0:T(8,128)S(1)}, f32[256,512]{1,0:T(8,128)S(1)}, u32[]{:S(2)}, u32[]{:S(2)}) collective-permute-start(f32[256,512]{1,0:T(8,128)S(1)} %convolution_bitcast_fusion.2), channel_id=1, source_target_pairs={{0,8},{8,0},{4,12},{12,4},{16,24},{24,16},{20,28},{28,20},{1,9},{9... | collective-permute-start | bytes 1572872 | tf_op jit(solution)/shard_map/ppermute | solution.py:14
  73.8 0.0 collective-permute-done.2
  73.9 0.1 broadcast_select_fusion.11
  74.0 1.1 %convolution_bitcast_fusion.5 = f32[256,512]{1,0:T(8,128)S(1)} fusion(f32[256,512]{1,0:T(8,128)S(1)} %get-tuple-element.12, f32[256,512]{1,0:T(8,128)S(1)} %get-tuple-element.11, f32[4,1,1,256,512]{4,3,2,1,0:T(8,128)S(1)} %copy-done), kind=kOutput, calls=%fused_computation.5 | convolution fusion | flops 805568512 | bytes 2097152 | tf_op jit(solution)/shard_map/dot_general | solution.py:18
  75.1 1.8 %collective-permute-start.3 = (f32[256,512]{1,0:T(8,128)S(1)}, f32[256,512]{1,0:T(8,128)S(1)}, u32[]{:S(2)}, u32[]{:S(2)}) collective-permute-start(f32[256,512]{1,0:T(8,128)S(1)} %convolution_bitcast_fusion.5), channel_id=1, source_target_pairs={{0,1},{1,0},{2,3},{3,2},{4,5},{5,4},{6,7},{7,6},{8,9},{9,8},{10,11... | collective-permute-start | bytes 1572872 | tf_op jit(solution)/shard_map/ppermute | solution.py:14
  76.9 8.2 %collective-permute-done.6 = f32[256,512]{1,0:T(8,128)S(1)} collective-permute-done((f32[256,512]{1,0:T(8,128)S(1)}, f32[256,512]{1,0:T(8,128)S(1)}, u32[]{:S(2)}, u32[]{:S(2)}) %collective-permute-start.6) | collective-permute-done | bytes 524320 | tf_op jit(solution)/shard_map/ppermute | solution.py:14
  85.1 0.1 broadcast_select_fusion.9
  85.2 1.1 %convolution_bitcast_fusion.1 = f32[256,512]{1,0:T(8,128)S(1)} fusion(f32[256,512]{1,0:T(8,128)S(1)} %get-tuple-element.19, f32[256,512]{1,0:T(8,128)S(1)} %get-tuple-element.18, f32[4,1,1,256,512]{4,3,2,1,0:T(8,128)S(1)} %copy-done), kind=kOutput, calls=%fused_computation.1 | convolution fusion | flops 805568512 | bytes 2097152 | tf_op jit(solution)/shard_map/dot_general | solution.py:18
  86.3 1.8 %collective-permute-start.7 = (f32[256,512]{1,0:T(8,128)S(1)}, f32[256,512]{1,0:T(8,128)S(1)}, u32[]{:S(2)}, u32[]{:S(2)}) collective-permute-start(f32[256,512]{1,0:T(8,128)S(1)} %convolution_bitcast_fusion.1), channel_id=1, source_target_pairs={{0,1},{1,0},{2,3},{3,2},{4,5},{5,4},{6,7},{7,6},{8,9},{9,8},{10,11... | collective-permute-start | bytes 1572872 | tf_op jit(solution)/shard_map/ppermute | solution.py:14
  88.1 0.0 collective-permute-done.3
  88.1 0.1 broadcast_select_fusion.15
  88.3 1.8 %convolution_bitcast_fusion.4 = f32[256,512]{0,1:T(8,128)S(1)} fusion(f32[256,512]{1,0:T(8,128)S(1)} %get-tuple-element.10, f32[256,512]{1,0:T(8,128)S(1)} %get-tuple-element.9, f32[4,1,1,256,512]{4,3,2,1,0:T(8,128)S(1)} %copy-done), kind=kOutput, calls=%fused_computation.4 | convolution fusion | flops 805568512 | bytes 2097152 | tf_op jit(solution)/shard_map/dot_general | solution.py:18
  90.1 9.3 %collective-permute-done.7 = f32[256,512]{1,0:T(8,128)S(1)} collective-permute-done((f32[256,512]{1,0:T(8,128)S(1)}, f32[256,512]{1,0:T(8,128)S(1)}, u32[]{:S(2)}, u32[]{:S(2)}) %collective-permute-start.7) | collective-permute-done | bytes 524320 | tf_op jit(solution)/shard_map/ppermute | solution.py:14
  99.4 0.1 broadcast_select_fusion.13
  99.5 1.8 %convolution_bitcast_fusion = f32[256,512]{0,1:T(8,128)S(1)} fusion(f32[256,512]{1,0:T(8,128)S(1)} %get-tuple-element.17, f32[256,512]{1,0:T(8,128)S(1)} %get-tuple-element.16, f32[4,1,1,256,512]{4,3,2,1,0:T(8,128)S(1)} %copy-done), kind=kOutput, calls=%fused_computation | convolution fusion | flops 805568512 | bytes 2097152 | tf_op jit(solution)/shard_map/dot_general | solution.py:18
  101.3 0.1 maximum_bitcast_fusion
  101.4 1.3 %copy.3 = f32[1,1,256,1024]{3,2,1,0:T(8,128)} copy(f32[1,1,256,1024]{2,3,1,0:T(8,128)S(1)} %maximum_bitcast_fusion) | data formatting | bytes 2097152 | tf_op jit(solution)/shard_map/broadcast_in_dim | solution.py:60
Async XLA Ops:
  0.0 21.6 %copy-start = (f32[4,1,1,256,512]{4,3,2,1,0:T(8,128)S(1)}, f32[4,1,1,256,512]{4,3,2,1,0:T(8,128)}, u32[]{:S(2)}) copy-start(f32[4,1,1,256,512]{4,3,2,1,0:T(8,128)} %param.3) | copy-start | bytes 6291460
  2.0 15.2 %collective-permute-start = (f32[256,512]{1,0:T(8,128)}, f32[256,512]{1,0:T(8,128)}, u32[]{:S(2)}, u32[]{:S(2)}) collective-permute-start(f32[256,512]{1,0:T(8,128)} %slice.32), channel_id=1, source_target_pairs={{0,16},{16,0},{4,20},{20,4},{8,24},{24,8},{12,28},{28,12},{1,17},{... | collective-permute-start | bytes 1572872 | tf_op jit(solution)/shard_map/ppermute | solution.py:14
  5.0 28.3 %copy-start.1 = (f32[1,1,256,1024]{3,2,1,0:T(8,128)S(1)}, f32[1,1,256,1024]{3,2,1,0:T(8,128)}, u32[]{:S(2)}) copy-start(f32[1,1,256,1024]{3,2,1,0:T(8,128)} %param.2) | copy-start | bytes 3145732
  19.8 13.4 %collective-permute-start.4 = (f32[256,512]{1,0:T(8,128)}, f32[256,512]{1,0:T(8,128)}, u32[]{:S(2)}, u32[]{:S(2)}) collective-permute-start(f32[256,512]{1,0:T(8,128)} %get-tuple-element.15), channel_id=1, source_target_pairs={{0,16},{16,0},{4,20},{20,4},{8,24},{24,8},{12,28},{28,12},{1,17},{... | collective-permute-start | bytes 1572872 | tf_op jit(solution)/shard_map/ppermute | solution.py:14
  23.9 37.1 %collective-permute-start.1 = (f32[256,512]{1,0:T(8,128)S(1)}, f32[256,512]{1,0:T(8,128)S(1)}, u32[]{:S(2)}, u32[]{:S(2)}) collective-permute-start(f32[256,512]{1,0:T(8,128)S(1)} %convolution_bitcast_fusion.7), channel_id=1, source_target_pairs={{0,2},{2,0},{1,3},{3,1},{4,6},{6,4},{5,7},{7,5},{8,10},{10,8},{9,1... | collective-permute-start | bytes 1572872 | tf_op jit(solution)/shard_map/ppermute | solution.py:14
  35.5 35.5 %collective-permute-start.5 = (f32[256,512]{1,0:T(8,128)S(1)}, f32[256,512]{1,0:T(8,128)S(1)}, u32[]{:S(2)}, u32[]{:S(2)}) collective-permute-start(f32[256,512]{1,0:T(8,128)S(1)} %convolution_bitcast_fusion.3), channel_id=1, source_target_pairs={{0,2},{2,0},{1,3},{3,1},{4,6},{6,4},{5,7},{7,5},{8,10},{10,8},{9,1... | collective-permute-start | bytes 1572872 | tf_op jit(solution)/shard_map/ppermute | solution.py:14
  62.2 11.7 %collective-permute-start.2 = (f32[256,512]{1,0:T(8,128)S(1)}, f32[256,512]{1,0:T(8,128)S(1)}, u32[]{:S(2)}, u32[]{:S(2)}) collective-permute-start(f32[256,512]{1,0:T(8,128)S(1)} %convolution_bitcast_fusion.6), channel_id=1, source_target_pairs={{0,8},{8,0},{4,12},{12,4},{16,24},{24,16},{20,28},{28,20},{1,9},{9... | collective-permute-start | bytes 1572872 | tf_op jit(solution)/shard_map/ppermute | solution.py:14
  72.3 12.8 %collective-permute-start.6 = (f32[256,512]{1,0:T(8,128)S(1)}, f32[256,512]{1,0:T(8,128)S(1)}, u32[]{:S(2)}, u32[]{:S(2)}) collective-permute-start(f32[256,512]{1,0:T(8,128)S(1)} %convolution_bitcast_fusion.2), channel_id=1, source_target_pairs={{0,8},{8,0},{4,12},{12,4},{16,24},{24,16},{20,28},{28,20},{1,9},{9... | collective-permute-start | bytes 1572872 | tf_op jit(solution)/shard_map/ppermute | solution.py:14
  75.1 13.1 %collective-permute-start.3 = (f32[256,512]{1,0:T(8,128)S(1)}, f32[256,512]{1,0:T(8,128)S(1)}, u32[]{:S(2)}, u32[]{:S(2)}) collective-permute-start(f32[256,512]{1,0:T(8,128)S(1)} %convolution_bitcast_fusion.5), channel_id=1, source_target_pairs={{0,1},{1,0},{2,3},{3,2},{4,5},{5,4},{6,7},{7,6},{8,9},{9,8},{10,11... | collective-permute-start | bytes 1572872 | tf_op jit(solution)/shard_map/ppermute | solution.py:14
  86.3 13.1 %collective-permute-start.7 = (f32[256,512]{1,0:T(8,128)S(1)}, f32[256,512]{1,0:T(8,128)S(1)}, u32[]{:S(2)}, u32[]{:S(2)}) collective-permute-start(f32[256,512]{1,0:T(8,128)S(1)} %convolution_bitcast_fusion.1), channel_id=1, source_target_pairs={{0,1},{1,0},{2,3},{3,2},{4,5},{5,4},{6,7},{7,6},{8,9},{9,8},{10,11... | collective-permute-start | bytes 1572872 | tf_op jit(solution)/shard_map/ppermute | solution.py:14
where the time goes:
time: 103 us
  waiting for transfers between devices  66.7 us (65%)
  starting transfers between devices  16.7 us (16%)
  matrix products  11.3 us (11%)
  other arithmetic  4.53 us (4%)
  local copies, waits for them, and re-layouts  3.33 us (3%)
    ppermute x8, waiting for transfers between devices, partner_2(): return lax.ppermute(block, axis, route)  66.7 us
    ppermute x8, starting transfers between devices, partner_2(): return lax.ppermute(block, axis, route)  16.7 us
    dot_general x8, matrix products, matmul(): jnp.dot(left, right, preferred_element_type=jnp.float32, precision=lax.Pr...  11.3 us
    select_n x8, other arithmetic, one_level(): lower_block = jnp.where(upper_bit == 0, state, partner)  4.46 us
  transfers between devices with their start and end apart: 8, of which 6 were waited for; matrix products, arithmetic and copies ran while one was open for 11% of the time, Pallas kernels for 0%

commit v1 on v0

v1 whole, which is shorter than its diff:
```python
import functools

import jax
import jax.numpy as jnp
from jax import lax
from jax.experimental import pallas as pl
from jax.experimental.pallas import tpu as pltpu
from jax.sharding import PartitionSpec as P

MESH = pl.DeviceIdType.MESH
WIDTH = 128
LEAD = 2


def high_low(x):
    high = x.astype(jnp.bfloat16)
    low = (x - high.astype(jnp.float32)).astype(jnp.bfloat16)
    return high, low


def right_side(x):
    high, low = high_low(x)
    return jnp.concatenate([high, low, high], axis=0)


def product(left, x):
    return jnp.dot(left, right_side(x), preferred_element_type=jnp.float32)


def kernel(plan, coef, blocks, out, state, got, raw, left, result,
           coef_sem, raw_sem, out_sem, send_sem, recv_sem):
    levels, chunks, rank, width = state.shape
    position = {"gx": lax.axis_index("gx"), "gy": lax.axis_index("gy")}
    upper, partner = [], []
    for axis, bit in plan:
        at = position[axis]
        one = lax.rem(at // (1 << bit), 2)
        upper.append(one)
        there = at + (1 - 2 * one) * (1 << bit)
        partner.append(
            (there, position["gy"]) if axis == "gx" else (position["gx"], there)
        )

    def columns(c):
        return pl.ds(pl.multiple_of(c * width, width), width)

    def load(c):
        return pltpu.make_async_copy(coef.at[:, columns(c)], state.at[0, c], coef_sem.at[c])

    def load_blocks(l):
        return pltpu.make_async_copy(blocks.at[l], raw.at[l], raw_sem.at[l])

    def send(l, c):
        return pltpu.make_async_remote_copy(
            src_ref=state.at[l, c],
            dst_ref=got.at[l, c],
            send_sem=send_sem.at[l, c],
            recv_sem=recv_sem.at[l, c],
            device_id=partner[l],
            device_id_type=MESH,
        )

    def store(c):
        return pltpu.make_async_copy(result.at[c], out.at[:, columns(c)], out_sem.at[c])

    for c in range(chunks):
        load(c).start()
    for l in range(levels):
        load_blocks(l).start()

    barrier = pltpu.get_barrier_semaphore()
    for l in range(levels):
        pl.semaphore_signal(barrier, inc=1, device_id=partner[l], device_id_type=MESH)
    pl.semaphore_wait(barrier, levels)

    for c in range(chunks):
        load(c).wait()
        send(0, c).start()

    for l in range(levels):
        load_blocks(l).wait()
        for j in range(2):
            half = upper[l] if j == 0 else 1 - upper[l]
            part = raw[l, :, pl.ds(pl.multiple_of(half * rank, rank), rank)]
            high, low = high_low(part)
            left[l, j] = jnp.concatenate([high, high, low], axis=1)

    def stage(l, c):
        own = product(left[l, 0], state[l, c])
        send(l, c).wait_recv()
        new = own + product(left[l, 1], got[l, c])
        if l + 1 < levels:
            state[l + 1, c] = new
            send(l + 1, c).start()
        else:
            result[c] = new
            store(c).start()

    def tick(t, carry):
        for l in range(levels):
            c = t - (0 if l == 0 else LEAD + l - 1)

            @pl.when(jnp.logical_and(c >= 0, c < chunks))
            def _(l=l, c=c):
                stage(l, c)

        return carry

    lax.fori_loop(0, chunks + LEAD + levels - 2, tick, 0)

    def finish(c, carry):
        for l in range(levels):
            send(l, c).wait_send()
        store(c).wait()
        return carry

    lax.fori_loop(0, chunks, finish, 0)


def on_device(coefficients, transfer_blocks):
    coef = coefficients[0, 0]
    blocks = transfer_blocks.reshape((transfer_blocks.shape[0],) + transfer_blocks.shape[3:])
    levels, rank, _ = blocks.shape
    total = coef.shape[1]
    chunks = total // WIDTH
    high_top = lax.axis_size("gx").bit_length() - 2
    low_top = lax.axis_size("gy").bit_length() - 2
    plan = [("gx", high_top), ("gy", low_top), ("gx", high_top - 1), ("gy", low_top - 1)]
    slots = (levels, chunks, rank, WIDTH)
    out = pl.pallas_call(
        functools.partial(kernel, plan),
        out_shape=jax.ShapeDtypeStruct(coef.shape, jnp.float32),
        in_specs=[pl.BlockSpec(memory_space=pl.ANY)] * 2,
        out_specs=pl.BlockSpec(memory_space=pl.ANY),
        scratch_shapes=[
            pltpu.VMEM(slots, jnp.float32),
            pltpu.VMEM(slots, jnp.float32),
            pltpu.VMEM(blocks.shape, jnp.float32),
            pltpu.VMEM((levels, 2, rank, 3 * rank), jnp.bfloat16),
            pltpu.VMEM(slots[1:], jnp.float32),
            pltpu.SemaphoreType.DMA((chunks,)),
            pltpu.SemaphoreType.DMA((levels,)),
            pltpu.SemaphoreType.DMA((chunks,)),
            pltpu.SemaphoreType.DMA((levels, chunks)),
            pltpu.SemaphoreType.DMA((levels, chunks)),
        ],
        compiler_params=pltpu.CompilerParams(
            collective_id=0, has_side_effects=True, vmem_limit_bytes=40 * 1024 * 1024
        ),
        cost_estimate=pl.CostEstimate(
            flops=12 * levels * rank * rank * total,
            bytes_accessed=4 * (2 * coef.size + blocks.size),
            transcendentals=0,
        ),
    )(coef, blocks)
    return out[None, None]


def solution(mesh):
    in_specs = (P("gx", "gy", None, None), P(None, "gx", "gy", None, None))
    out_specs = P("gx", "gy", None, None)
    return jax.shard_map(
        on_device, mesh=mesh, in_specs=in_specs, out_specs=out_specs, check_vma=False
    )
```

time: 103 us -> 70.5 us (0.68)
  waiting for transfers between devices: 66.7 us -> 0 us
  Pallas kernels: 0 us -> 66.5 us
  starting transfers between devices: 16.7 us -> 0 us
  matrix products: 11.3 us -> 0 us
  other arithmetic: 4.53 us -> 0 us
    ppermute x8 -> x0, waiting for transfers between devices: 66.7 us -> none  [partner_2(): return lax.ppermute(block, axis, route)]
    pallas_call x0 -> x1, Pallas kernels: none -> 66.5 us  [on_device(): pl.pallas_call(functools.partial(kernel, plan), out_shape=jax.ShapeDtypeS...]
    ppermute x8 -> x0, starting transfers between devices: 16.7 us -> none  [partner_2(): return lax.ppermute(block, axis, route)]
    dot_general x8 -> x0, matrix products: 11.3 us -> none  [matmul(): jnp.dot(left, right, preferred_element_type=jnp.float32, precision=lax.Pr...]
    select_n x8 -> x0, other arithmetic: 4.46 us -> none  [one_level(): lower_block = jnp.where(upper_bit == 0, state, partner)]
    unnamed x4 -> x5, local copies, waits for them, and re-layouts: 0.01 us -> 3.79 us
    slice x1 -> x0, local copies, waits for them, and re-layouts: 2.02 us -> none  [on_device(): groups = [state[:, :width], state[:, width:]]]
    broadcast_in_dim x1 -> x0, local copies, waits for them, and re-layouts: 1.31 us -> none  [on_device(): return state[None, None]]
  transfers between devices with their start and end apart: 8 -> 0, of which waited for: 6 -> 0; matrix products, arithmetic and copies ran while one was open for 11% -> 0% of each run, Pallas kernels for 0% -> 0%
where the time goes in v1:
time: 70.5 us; the launch traced here: 70.3 us
  Pallas kernels  66.5 us (94%)
  local copies, waits for them, and re-layouts  3.79 us (5%)
    pallas_call x1, Pallas kernels, on_device(): pl.pallas_call(functools.partial(kernel, plan), out_shape=jax.ShapeDtypeS...  66.5 us
    unnamed x5, local copies, waits for them, and re-layouts  3.79 us

profile of v1, /device:TPU:0, one launch (start us, length us, event | category | flops | bytes accessed | tf_op | source)
XLA Modules:
  0.0 70.3 jit_solution(1407130894833741863)
XLA Ops:
  0.0 0.0 copy-start
  0.0 1.6 %copy-done = f32[4,1,1,256,512]{4,3,2,1,0:T(8,128)S(1)} copy-done((f32[4,1,1,256,512]{4,3,2,1,0:T(8,128)S(1)}, f32[4,1,1,256,512]{4,3,2,1,0:T(8,128)}, u32[]{:S(2)}) %copy-start) | copy-done | bytes 2097176
  1.6 0.0 copy-start.1
  1.6 1.2 %copy-done.1 = f32[1,1,256,1024]{3,2,1,0:T(8,128)S(1)} copy-done((f32[1,1,256,1024]{3,2,1,0:T(8,128)S(1)}, f32[1,1,256,1024]{3,2,1,0:T(8,128)}, u32[]{:S(2)}) %copy-start.1) | copy-done | bytes 1048600
  2.8 66.5 %shard_map.28 = f32[256,1024]{1,0:T(8,128)S(1)} custom-call(f32[256,1024]{1,0:T(8,128)S(1)} %bitcast.5, f32[4,256,512]{2,1,0:T(8,128)S(1)} %bitcast.4), custom_call_target="tpu_custom_call" | custom-call | flops 3221225472 | bytes 4194304 | tf_op jit(solution)/shard_map/pallas_call | solution.py:130
  69.4 1.0 %copy.4 = f32[1,1,256,1024]{3,2,1,0:T(8,128)} copy(f32[1,1,256,1024]{3,2,1,0:T(8,128)S(1)} %bitcast.3) | data formatting | bytes 2097152
Async XLA Ops:
  0.0 1.6 %copy-start = (f32[4,1,1,256,512]{4,3,2,1,0:T(8,128)S(1)}, f32[4,1,1,256,512]{4,3,2,1,0:T(8,128)}, u32[]{:S(2)}) copy-start(f32[4,1,1,256,512]{4,3,2,1,0:T(8,128)} %param.3) | copy-start | bytes 6291460
  1.6 1.2 %copy-start.1 = (f32[1,1,256,1024]{3,2,1,0:T(8,128)S(1)}, f32[1,1,256,1024]{3,2,1,0:T(8,128)}, u32[]{:S(2)}) copy-start(f32[1,1,256,1024]{3,2,1,0:T(8,128)} %param.2) | copy-start | bytes 3145732

commit v2 on v1

--- a/solution.py
+++ b/solution.py
@@ -9,7 +9,8 @@
 
 MESH = pl.DeviceIdType.MESH
 WIDTH = 128
-LEAD = 2
+LAG = (0, 2, 3, 5)
+AHEAD = 2
 
 
 def high_low(x):
@@ -73,17 +74,19 @@
         pl.semaphore_signal(barrier, inc=1, device_id=partner[l], device_id_type=MESH)
     pl.semaphore_wait(barrier, levels)
 
-    for c in range(chunks):
-        load(c).wait()
-        send(0, c).start()
-
-    for l in range(levels):
+    def prepare(l):
         load_blocks(l).wait()
         for j in range(2):
             half = upper[l] if j == 0 else 1 - upper[l]
             part = raw[l, :, pl.ds(pl.multiple_of(half * rank, rank), rank)]
             high, low = high_low(part)
             left[l, j] = jnp.concatenate([high, high, low], axis=1)
+
+    for c in range(chunks):
+        load(c).wait()
+        if c < AHEAD:
+            send(0, c).start()
+    prepare(0)
 
     def stage(l, c):
         own = product(left[l, 0], state[l, c])
@@ -98,15 +101,22 @@
 
     def tick(t, carry):
         for l in range(levels):
-            c = t - (0 if l == 0 else LEAD + l - 1)
+            c = t - LAG[l]
 
             @pl.when(jnp.logical_and(c >= 0, c < chunks))
             def _(l=l, c=c):
                 stage(l, c)
+                if l == 0 and AHEAD < chunks:
 
+                    @pl.when(t + AHEAD < chunks)
+                    def _():
+                        send(0, t + AHEAD).start()
+
+        for l in range(1, levels):
+            pl.when(t == l - 1)(functools.partial(prepare, l))
         return carry
 
-    lax.fori_loop(0, chunks + LEAD + levels - 2, tick, 0)
+    lax.fori_loop(0, chunks + LAG[-1], tick, 0)
 
     def finish(c, carry):
         for l in range(levels):
@@ -145,7 +155,7 @@
             pltpu.SemaphoreType.DMA((levels, chunks)),
         ],
         compiler_params=pltpu.CompilerParams(
-            collective_id=0, has_side_effects=True, vmem_limit_bytes=40 * 1024 * 1024
+            collective_id=0, has_side_effects=True, vmem_limit_bytes=60 * 1024 * 1024
         ),
         cost_estimate=pl.CostEstimate(
             flops=12 * levels * rank * rank * total,

time: 70.5 us -> 68.1 us (0.966)
  local copies, waits for them, and re-layouts: 3.79 us -> 2.31 us
  Pallas kernels: 66.5 us -> 65.7 us
    unnamed x5 -> x1, local copies, waits for them, and re-layouts: 3.79 us -> 2.31 us
    pallas_call x1, Pallas kernels: 66.5 us -> 65.7 us  [on_device(): pl.pallas_call(functools.partial(kernel, plan), out_shape=jax.ShapeDtypeS...]
where the time goes in v2:
time: 68.1 us; the launch traced here: 68 us
  Pallas kernels  65.7 us (96%)
  local copies, waits for them, and re-layouts  2.31 us (3%)
    pallas_call x1, Pallas kernels, on_device(): pl.pallas_call(functools.partial(kernel, plan), out_shape=jax.ShapeDtypeS...  65.7 us
    unnamed x1, local copies, waits for them, and re-layouts  2.31 us

profile of v2, /device:TPU:0, one launch (start us, length us, event | category | flops | bytes accessed | tf_op | source)
XLA Modules:
  0.0 68.0 jit_solution(13932701279449005064)
XLA Ops:
  0.0 65.7 %shard_map.28 = f32[256,1024]{1,0:T(8,128)} custom-call(f32[256,1024]{1,0:T(8,128)} %bitcast.5, f32[4,256,512]{2,1,0:T(8,128)} %bitcast.4), custom_call_target="tpu_custom_call" | custom-call | flops 3221225472 | bytes 4194304 | tf_op jit(solution)/shard_map/pallas_call | solution.py:140
  65.7 2.3 %copy.4 = f32[1,1,256,1024]{3,2,1,0:T(8,128)} copy(f32[1,1,256,1024]{3,2,1,0:T(8,128)} %bitcast.3) | data formatting | bytes 2097152

commit v3 on v2

--- a/solution.py
+++ b/solution.py
@@ -155,7 +155,7 @@
             pltpu.SemaphoreType.DMA((levels, chunks)),
         ],
         compiler_params=pltpu.CompilerParams(
-            collective_id=0, has_side_effects=True, vmem_limit_bytes=60 * 1024 * 1024
+            collective_id=0, has_side_effects=True, vmem_limit_bytes=52 * 1024 * 1024
         ),
         cost_estimate=pl.CostEstimate(
             flops=12 * levels * rank * rank * total,

time: 68.1 us -> 66.2 us (0.972)
  local copies, waits for them, and re-layouts: 2.31 us -> 0.97 us
    unnamed x1, local copies, waits for them, and re-layouts: 2.31 us -> 0.97 us
where the time goes in v3:
time: 66.2 us; the launch traced here: 66.1 us
  Pallas kernels  65.1 us (98%)
  local copies, waits for them, and re-layouts  0.97 us (1%)
    pallas_call x1, Pallas kernels, on_device(): pl.pallas_call(functools.partial(kernel, plan), out_shape=jax.ShapeDtypeS...  65.1 us

profile of v3, /device:TPU:0, one launch (start us, length us, event | category | flops | bytes accessed | tf_op | source)
XLA Modules:
  0.0 66.1 jit_solution(8892946066438553501)
XLA Ops:
  0.0 65.1 %shard_map.28 = f32[256,1024]{1,0:T(8,128)S(1)} custom-call(f32[256,1024]{1,0:T(8,128)} %bitcast.5, f32[4,256,512]{2,1,0:T(8,128)} %bitcast.4), custom_call_target="tpu_custom_call" | custom-call | flops 3221225472 | bytes 4194304 | tf_op jit(solution)/shard_map/pallas_call | solution.py:140
  65.1 1.0 %copy.4 = f32[1,1,256,1024]{3,2,1,0:T(8,128)} copy(f32[1,1,256,1024]{3,2,1,0:T(8,128)S(1)} %bitcast.3) | data formatting | bytes 2097152

commit v4 on v3

--- a/solution.py
+++ b/solution.py
@@ -64,14 +64,13 @@
     def store(c):
         return pltpu.make_async_copy(result.at[c], out.at[:, columns(c)], out_sem.at[c])
 
+    barrier = pltpu.get_barrier_semaphore()
+    for l in range(levels):
+        pl.semaphore_signal(barrier, inc=1, device_id=partner[l], device_id_type=MESH)
     for c in range(chunks):
         load(c).start()
     for l in range(levels):
         load_blocks(l).start()
-
-    barrier = pltpu.get_barrier_semaphore()
-    for l in range(levels):
-        pl.semaphore_signal(barrier, inc=1, device_id=partner[l], device_id_type=MESH)
     pl.semaphore_wait(barrier, levels)
 
     def prepare(l):
@@ -82,11 +81,12 @@
             high, low = high_low(part)
             left[l, j] = jnp.concatenate([high, high, low], axis=1)
 
-    for c in range(chunks):
+    for c in range(AHEAD):
         load(c).wait()
-        if c < AHEAD:
-            send(0, c).start()
+        send(0, c).start()
     prepare(0)
+    for c in range(AHEAD, chunks):
+        load(c).wait()
 
     def stage(l, c):
         own = product(left[l, 0], state[l, c])

time: 66.2 us -> 66.2 us (level)
  no operation moved by 1% of the time
where the time goes in v4:
time: 66.2 us; the launch traced here: 66.1 us
  Pallas kernels  65.1 us (98%)
  local copies, waits for them, and re-layouts  0.97 us (1%)
    pallas_call x1, Pallas kernels, on_device(): pl.pallas_call(functools.partial(kernel, plan), out_shape=jax.ShapeDtypeS...  65.1 us

profile of v4, /device:TPU:0, one launch (start us, length us, event | category | flops | bytes accessed | tf_op | source)
XLA Modules:
  0.0 66.1 jit_solution(15502120738772711034)
XLA Ops:
  0.0 65.1 %shard_map.28 = f32[256,1024]{1,0:T(8,128)S(1)} custom-call(f32[256,1024]{1,0:T(8,128)} %bitcast.5, f32[4,256,512]{2,1,0:T(8,128)} %bitcast.4), custom_call_target="tpu_custom_call" | custom-call | flops 3221225472 | bytes 4194304 | tf_op jit(solution)/shard_map/pallas_call | solution.py:140
  65.1 1.0 %copy.4 = f32[1,1,256,1024]{3,2,1,0:T(8,128)} copy(f32[1,1,256,1024]{3,2,1,0:T(8,128)S(1)} %bitcast.3) | data formatting | bytes 2097152
